TPU v7x, 32 devices: a whole 2x2x4 slice. The times are simulated.
32 devices in a mesh: comp: 4 (over y, x), dom: 8 (over z, core).
Axes of the slice: x: 2, y: 2, z: 4, core: 2. Of those that a mesh axis runs over, the one named last changes fastest.
Arguments:
- model_state: bfloat16 [4, 1024, 48, 128], P('comp', 'dom'), may hold values from -6 to 6
- coefficient: bfloat16 [4, 1024, 48, 128], P('comp', 'dom'), may hold values from 0.049804688 to 0.5
- stencil_blocks: bfloat16 [4, 7, 128, 128], P('comp'), may hold values from -0.1875 to 0.1875
- neighbours: int32 [4, 1024, 7], P('comp', 'dom'), may hold values from 0 to 191
- land_mask: int32 [1024, 128], P('dom'), may hold values 0 or 1
- surface_flux: bfloat16 [4, 1024, 20, 128], P('comp', 'dom'), may hold values from -6 to 6
- remap_pairs: int32 [4, 1024, 2], P('comp', 'dom'), may hold values from 0 to 4095, as said below
- remap_weights: bfloat16 [4, 1024, 2, 128, 128], P('comp', 'dom'), may hold values from -0.5 to 0.5
Outputs:
- next_state: bfloat16 [4, 1024, 48, 128], P('comp', 'dom')
- remapped: bfloat16 [4, 1024, 20, 128], P('comp', 'dom')
Inputs may be any that keep to these rules, and one draw needn't show every extreme that they name: `remap_pairs`: tiles of sections 0 to 2 name tiles of section 3, tiles of section 3 name tiles of sections 0 to 2. The 256 entries of one device name tiles of one dom index at most 32 times, and exactly 32 times for some dom index.
All inputs are finite; a program needn't handle non-finite values. No bound on the sum of `land_mask` on one device may be relied on, other than what follows from the above.
Results may differ from a plain program's by a relative error of at most 0.0075.
Values may be sent and summed in bfloat16 or wider, within the bound.
A program may use at most 128 MiB of HBM per device.

v0:
```python
import functools

import jax
import jax.numpy as jnp
import numpy as np
from jax import lax
from jax.experimental import pallas as pl
from jax.experimental.pallas import tpu as pltpu
from jax.sharding import PartitionSpec as P

STEPS = 5
GROUP = 16
MESH = pl.DeviceIdType.MESH


def coupled_kernel(
    n_dom,
    n_sec,
    cap,
    near_ref,
    entry_ref,
    state_hbm,
    coef_hbm,
    flux_hbm,
    weight_hbm,
    stencil_ref,
    mask_ref,
    code_ref,
    perm_ref,
    next_ref,
    remap_ref,
    buf0,
    buf1,
    buf2,
    buf3,
    buf4,
    coef_ref,
    flux_ref,
    weight_ref,
    lhs_ref,
    out_pieces,
    in_pieces,
    in_codes,
    hit_ref,
    part_ref,
    recv_ref,
    local_sem,
    halo_send,
    halo_recv,
    piece_send,
    piece_recv,
    code_send,
    code_recv,
    part_send,
    part_recv,
):
    bufs = (buf0, buf1, buf2, buf3, buf4)
    tiles, levels, cells = coef_ref.shape
    field_count = flux_ref.shape[1]
    slots_near = near_ref.shape[0] // tiles
    per_tile = weight_ref.shape[0] // tiles
    rim = tiles // 4
    sec = lax.axis_index("comp")
    dom = lax.axis_index("dom")
    last = n_sec - 1
    up = lax.rem(dom + 1, n_dom)
    down = lax.rem(dom + n_dom - 1, n_dom)

    loads = (
        pltpu.make_async_copy(state_hbm, buf0.at[pl.ds(rim, tiles)], local_sem.at[0]),
        pltpu.make_async_copy(flux_hbm, flux_ref, local_sem.at[1]),
        pltpu.make_async_copy(weight_hbm, weight_ref, local_sem.at[2]),
        pltpu.make_async_copy(coef_hbm, coef_ref, local_sem.at[3]),
    )
    for load in loads:
        load.start()

    barrier = pltpu.get_barrier_semaphore()
    for k in range(1, n_dom):
        pl.semaphore_signal(
            barrier, inc=1, device_id=(sec, lax.rem(dom + k, n_dom)), device_id_type=MESH
        )
    for k in range(1, n_sec):
        pl.semaphore_signal(
            barrier, inc=1, device_id=(lax.rem(sec + k, n_sec), dom), device_id_type=MESH
        )
    pl.semaphore_wait(barrier, n_dom - 1 + n_sec - 1)

    def halo(step, side):
        if step == 0:
            source, base = state_hbm, 0
        else:
            source, base = bufs[step], rim
        if side == 0:
            src = source.at[pl.ds(base, rim)]
            dst = bufs[step].at[pl.ds(rim + tiles, rim)]
            target = down
        else:
            src = source.at[pl.ds(base + tiles - rim, rim)]
            dst = bufs[step].at[pl.ds(0, rim)]
            target = up
        return pltpu.make_async_remote_copy(
            src_ref=src,
            dst_ref=dst,
            send_sem=halo_send.at[step, side],
            recv_sem=halo_recv.at[step, side],
            device_id=(sec, target),
            device_id_type=MESH,
        )

    def piece_copy(k):
        target = lax.rem(dom + k, n_dom)
        return pltpu.make_async_remote_copy(
            src_ref=out_pieces.at[k],
            dst_ref=in_pieces.at[dom],
            send_sem=piece_send.at[k],
            recv_sem=piece_recv.at[k],
            device_id=(sec, target),
            device_id_type=MESH,
        )

    def code_copy(k):
        target = lax.rem(dom + k, n_dom)
        return pltpu.make_async_remote_copy(
            src_ref=code_ref.at[target],
            dst_ref=in_codes.at[dom],
            send_sem=code_send.at[k],
            recv_sem=code_recv.at[k],
            device_id=(sec, target),
            device_id_type=MESH,
        )

    for side in range(2):
        halo(0, side).start()
    for k in range(1, n_dom):
        code_copy(k).start()
    in_codes[dom] = code_ref[dom]
    loads[0].wait()
    loads[1].wait()

    def add_surface(block, carry):
        start = block * 8
        own = buf0[pl.ds(rim + start, 8)].astype(jnp.float32)[:, :field_count]
        mixed = flux_ref[pl.ds(start, 8)].astype(jnp.float32) + own
        flux_ref[pl.ds(start, 8)] = mixed.astype(jnp.bfloat16)
        return carry

    lax.fori_loop(0, tiles // 8, add_surface, 0)
    loads[2].wait()

    def make_pieces(target, chunk, store):
        rows = []
        for i in range(16):
            entry = entry_ref[target * cap + chunk * 16 + i]
            rows.append(
                jnp.dot(
                    flux_ref[entry // per_tile],
                    weight_ref[entry],
                    preferred_element_type=jnp.float32,
                )
            )
        stacked = jnp.concatenate(rows, axis=0).astype(jnp.bfloat16)
        sorted_rows = jnp.dot(perm_ref[...], stacked, preferred_element_type=jnp.float32)
        store(chunk, sorted_rows.astype(jnp.bfloat16).reshape(field_count, 16, cells))

    def send_pieces(k, carry):
        target = lax.rem(dom + k, n_dom)

        def store(chunk, value):
            out_pieces[k, :, pl.ds(pl.multiple_of(chunk * 16, 16), 16), :] = value

        def body(chunk, inner):
            make_pieces(target, chunk, store)
            return inner

        lax.fori_loop(0, cap // 16, body, 0)
        piece_copy(k).start()
        return carry

    lax.fori_loop(1, n_dom, send_pieces, 0)

    def own_body(chunk, inner):
        def store(at, value):
            in_pieces[dom, :, pl.ds(pl.multiple_of(at * 16, 16), 16), :] = value

        make_pieces(dom, chunk, store)
        return inner

    lax.fori_loop(0, cap // 16, own_body, 0)
    loads[3].wait()

    def advance(step, first, count):
        source = bufs[step]

        def body(group, carry):
            start = group * GROUP
            for i in range(GROUP):
                for k in range(slots_near):
                    lhs_ref[i * levels : (i + 1) * levels, k * cells : (k + 1) * cells] = source[
                        near_ref[(start + i) * slots_near + k]
                    ]
            summed = jnp.dot(lhs_ref[...], stencil_ref[...], preferred_element_type=jnp.float32)
            summed = summed.reshape(GROUP, levels, cells)
            start = pl.multiple_of(start, GROUP)
            own = source[pl.ds(rim + start, GROUP)].astype(jnp.float32)
            local_coef = coef_ref[pl.ds(start, GROUP)].astype(jnp.float32)
            wet = mask_ref[pl.ds(start, GROUP), :].astype(jnp.float32)
            factor = jnp.where(sec == last, wet, jnp.float32(1.0))
            value = ((own + local_coef * summed) * factor[:, None, :]).astype(jnp.bfloat16)
            if step == STEPS - 1:
                next_ref[pl.ds(start, GROUP)] = value
            else:
                bufs[step + 1][pl.ds(rim + start, GROUP)] = value
            return carry

        lax.fori_loop(first // GROUP, (first + count) // GROUP, body, 0)

    def part_copy(place, slot, target):
        return pltpu.make_async_remote_copy(
            src_ref=part_ref.at[place],
            dst_ref=recv_ref.at[slot],
            send_sem=part_send.at[place],
            recv_sem=part_recv.at[slot],
            device_id=(target, dom),
            device_id_type=MESH,
        )

    def partial_sums(place, target):
        codes = jnp.sum(in_codes[...], axis=0)[0:1, :]
        wanted = target * tiles + lax.broadcasted_iota(jnp.int32, hit_ref.shape, 0)
        hit_ref[...] = (codes == wanted).astype(jnp.float32).astype(jnp.bfloat16)

        def body(field, carry):
            arrived = in_pieces[:, field].reshape(n_dom * cap, cells)
            part_ref[place, field] = jnp.dot(
                hit_ref[...], arrived, preferred_element_type=jnp.float32
            ).astype(jnp.bfloat16)
            return carry

        lax.fori_loop(0, field_count, body, 0)

    def exchange_sections():
        for k in range(1, n_dom):
            piece_copy(k).wait()
            code_copy(k).wait()

        @pl.when(sec != last)
        def _():
            partial_sums(0, last)
            part_copy(0, sec, last).start()

        @pl.when(sec == last)
        def _():
            for target in range(last):
                partial_sums(target, target)
                part_copy(target, 0, target).start()

    for step in range(STEPS):
        for side in range(2):
            halo(step, side).wait()
        if step < STEPS - 1:
            advance(step, 0, rim)
            halo(step + 1, 0).start()
            advance(step, tiles - rim, rim)
            halo(step + 1, 1).start()
            advance(step, rim, tiles - 2 * rim)
        else:
            advance(step, 0, tiles)
        if step == 0:
            exchange_sections()

    @pl.when(sec != last)
    def _():
        part_copy(0, sec, last).wait_send()
        part_copy(0, 0, last).wait_recv()

        def body(field, carry):
            remap_ref[field] = recv_ref[0, field]
            return carry

        lax.fori_loop(0, field_count, body, 0)

    @pl.when(sec == last)
    def _():
        for place in range(last):
            part_copy(place, place, place).wait()

        def body(field, carry):
            total = recv_ref[0, field].astype(jnp.float32)
            for place in range(1, last):
                total = total + recv_ref[place, field].astype(jnp.float32)
            remap_ref[field] = total.astype(jnp.bfloat16)
            return carry

        lax.fori_loop(0, field_count, body, 0)


def slot_tables(pairs, tiles, n_dom, n_sec, cap):
    total = pairs.size
    targets = pairs.reshape(total)
    column = targets // tiles % n_dom
    local_code = targets // (n_dom * tiles) * tiles + targets % tiles
    order = jnp.arange(total, dtype=jnp.int32)
    earlier = (column[:, None] == column[None, :]) & (order[None, :] < order[:, None])
    placed = column * cap + jnp.sum(earlier.astype(jnp.int32), axis=1)
    slot_count = n_dom * cap
    hit = jnp.arange(slot_count, dtype=jnp.int32)[:, None] == placed[None, :]
    packed = order * (2 * n_sec * tiles) + local_code + 1
    found = jnp.sum(jnp.where(hit, packed[None, :], 0), axis=1)
    entry = found // (2 * n_sec * tiles)
    code = found % (2 * n_sec * tiles) - 1
    code = jnp.where(found == 0, n_sec * tiles, code).reshape(n_dom, 1, 1, cap)
    here = (jnp.arange(n_dom, dtype=jnp.int32) == lax.axis_index("dom"))[None, None, :, None]
    rows = jnp.where(here, code, 0).reshape(n_dom, 1, slot_count)
    return entry, jnp.broadcast_to(rows, (n_dom, 8, slot_count))


def local(
    model_state,
    coefficient,
    stencil_blocks,
    neighbours,
    land_mask,
    surface_flux,
    remap_pairs,
    remap_weights,
):
    n_dom = lax.axis_size("dom")
    n_sec = lax.axis_size("comp")
    _, tiles, levels, cells = model_state.shape
    field_count = surface_flux.shape[2]
    near = neighbours.shape[2]
    per_tile = remap_pairs.shape[2]
    total = tiles * per_tile
    cap = max(16, -(-total // n_dom))
    rim = tiles // 4
    entry, codes = slot_tables(remap_pairs[0], tiles, n_dom, n_sec, cap)
    rows = field_count * 16
    at = np.arange(rows)
    perm = np.zeros((rows, rows), np.float32)
    perm[at, (at % 16) * field_count + at // 16] = 1.0
    vmem = pl.BlockSpec(memory_space=pltpu.VMEM)
    smem = pl.BlockSpec(memory_space=pltpu.SMEM)
    anywhere = pl.BlockSpec(memory_space=pl.ANY)
    extended = pltpu.VMEM((tiles + 2 * rim, levels, cells), jnp.bfloat16)
    dma = pltpu.SemaphoreType.DMA
    next_state, remapped = pl.pallas_call(
        functools.partial(coupled_kernel, n_dom, n_sec, cap),
        out_shape=(
            jax.ShapeDtypeStruct((tiles, levels, cells), jnp.bfloat16),
            jax.ShapeDtypeStruct((field_count, tiles, cells), jnp.bfloat16),
        ),
        in_specs=[smem, smem] + [anywhere] * 4 + [vmem] * 4,
        out_specs=(vmem, vmem),
        scratch_shapes=[extended] * STEPS
        + [
            pltpu.VMEM((tiles, levels, cells), jnp.bfloat16),
            pltpu.VMEM((tiles, field_count, cells), jnp.bfloat16),
            pltpu.VMEM((total, cells, cells), jnp.bfloat16),
            pltpu.VMEM((GROUP * levels, near * cells), jnp.bfloat16),
            pltpu.VMEM((n_dom, field_count, cap, cells), jnp.bfloat16),
            pltpu.VMEM((n_dom, field_count, cap, cells), jnp.bfloat16),
            pltpu.VMEM((n_dom, 8, n_dom * cap), jnp.int32),
            pltpu.VMEM((tiles, n_dom * cap), jnp.bfloat16),
            pltpu.VMEM((n_sec - 1, field_count, tiles, cells), jnp.bfloat16),
            pltpu.VMEM((n_sec - 1, field_count, tiles, cells), jnp.bfloat16),
            dma((4,)),
            dma((STEPS, 2)),
            dma((STEPS, 2)),
            dma((n_dom,)),
            dma((n_dom,)),
            dma((n_dom,)),
            dma((n_dom,)),
            dma((n_sec - 1,)),
            dma((n_sec - 1,)),
        ],
        compiler_params=pltpu.CompilerParams(
            collective_id=0, has_side_effects=True, vmem_limit_bytes=56 * 2**20
        ),
    )(
        neighbours.reshape(tiles * near),
        entry,
        model_state[0],
        coefficient[0],
        surface_flux[0],
        remap_weights.reshape(total, cells, cells),
        stencil_blocks.reshape(near * cells, cells),
        land_mask,
        codes,
        jnp.asarray(perm, jnp.bfloat16),
    )
    return (next_state[None], remapped.transpose(1, 0, 2)[None])


def solution(mesh):
    placed = (
        P("comp", "dom", None, None),
        P("comp", "dom", None, None),
        P("comp", None, None, None),
        P("comp", "dom", None),
        P("dom", None),
        P("comp", "dom", None, None),
        P("comp", "dom", None),
        P("comp", "dom", None, None, None),
    )
    return jax.shard_map(
        local,
        mesh=mesh,
        in_specs=placed,
        out_specs=(P("comp", "dom", None, None), P("comp", "dom", None, None)),
        check_vma=False,
    )
```

profile of v0, /device:TPU:15, one launch (start us, length us, event | category | flops | bytes accessed | tf_op | source)
XLA Modules:
  0.0 109.1 jit_solution(4690594869441175994)
XLA Ops:
  0.6 0.1 broadcast_in_dim.63
  0.7 0.1 broadcast_in_dim.64
  0.8 0.8 copy.15
  1.6 0.8 reshape.203.near_ref
  2.4 0.8 copy.16
  3.2 0.1 reshape_squeeze.3
  3.3 0.2 convert_reduce_fusion
  3.5 0.1 select_reduce_fusion
  3.7 0.6 and_select_fusion.entry_ref
  4.3 0.1 reduce_sum.22
  4.3 0.1 broadcast_in_dim.68
  4.4 0.6 broadcast_in_dim.70.code_ref
  5.1 2.4 %copy.19 = bf16[1,128,20,128]{3,2,1,0:T(8,128)(2,1)} copy(bf16[1,128,20,128]{3,1,2,0:T(8,128)(2,1)} %param.14) | data formatting | bytes 1310720 | tf_op args[5]
  7.5 98.0 %shard_map.104 = (bf16[128,48,128]{2,1,0:T(8,128)(2,1)}, bf16[20,128,128]{2,1,0:T(8,128)(2,1)}) custom-call(s32[896]{0:T(1024)} %reshape.203.near_ref, s32[256]{0:T(256)} %and_select_fusion.entry_ref, bf16[128,48,128]{2,1,0:T(8,128)(2,1)} %bitcast.13, bf16[128,48,128]{2,1,0:T(8,128)(2,1)} %bitcast.14, bf16[128,20,128]{2,1,0:T(8,128)(2,1)} %bitcast.12, ...), custom_call_target="tpu_custom_call" | custom-call | tf_op jit(solution)/shard_map/pallas_call | solution.py:347
  105.5 0.0 copy-start
  105.5 2.7 %copy.22 = bf16[1,128,48,128]{3,2,1,0:T(8,128)(2,1)} copy(bf16[1,128,48,128]{3,2,1,0:T(8,128)(2,1)} %bitcast.15) | data formatting | bytes 3145728
  108.2 0.0 copy-done
  108.2 0.8 copy.23
  (6 shorter events, 0.1 us)
Async XLA Ops:
  105.5 2.7 %copy-start = (bf16[20,128,128]{2,1,0:T(8,128)(2,1)S(1)}, bf16[20,128,128]{2,1,0:T(8,128)(2,1)}, u32[]{:S(2)}) copy-start(bf16[20,128,128]{2,1,0:T(8,128)(2,1)} %get-tuple-element.5) | copy-start | bytes 1966084
where the time goes:
time: 110 us; the launch traced here: 109 us
  Pallas kernels  98 us (89%)
  local copies, waits for them, and re-layouts  9.43 us (9%)
    pallas_call x1, Pallas kernels, local(): pl.pallas_call(functools.partial(coupled_kernel, n_dom, n_sec, cap), out_...  98 us
    unnamed x7, local copies, waits for them, and re-layouts  7.54 us

commit v1 on v0

--- a/solution.py
+++ b/solution.py
@@ -10,6 +10,8 @@
 
 STEPS = 5
 GROUP = 16
+EDGE_PARTS = 2
+EARLY = 4
 MESH = pl.DeviceIdType.MESH
 
 
@@ -36,6 +38,7 @@
     buf4,
     coef_ref,
     flux_ref,
+    field_ref,
     weight_ref,
     lhs_ref,
     out_pieces,
@@ -56,7 +59,7 @@
 ):
     bufs = (buf0, buf1, buf2, buf3, buf4)
     tiles, levels, cells = coef_ref.shape
-    field_count = flux_ref.shape[1]
+    field_count = flux_ref.shape[0]
     slots_near = near_ref.shape[0] // tiles
     per_tile = weight_ref.shape[0] // tiles
     rim = tiles // 4
@@ -86,24 +89,26 @@
         )
     pl.semaphore_wait(barrier, n_dom - 1 + n_sec - 1)
 
-    def halo(step, side):
+    def halo(step, side, part, parts=EDGE_PARTS):
+        size = rim // parts
+        at = part * size
         if step == 0:
             source, base = state_hbm, 0
         else:
             source, base = bufs[step], rim
         if side == 0:
-            src = source.at[pl.ds(base, rim)]
-            dst = bufs[step].at[pl.ds(rim + tiles, rim)]
+            src = source.at[pl.ds(base + at, size)]
+            dst = bufs[step].at[pl.ds(rim + tiles + at, size)]
             target = down
         else:
-            src = source.at[pl.ds(base + tiles - rim, rim)]
-            dst = bufs[step].at[pl.ds(0, rim)]
+            src = source.at[pl.ds(base + tiles - rim + at, size)]
+            dst = bufs[step].at[pl.ds(at, size)]
             target = up
         return pltpu.make_async_remote_copy(
             src_ref=src,
             dst_ref=dst,
-            send_sem=halo_send.at[step, side],
-            recv_sem=halo_recv.at[step, side],
+            send_sem=halo_send.at[step, side * parts + part],
+            recv_sem=halo_recv.at[step, side * parts + part],
             device_id=(sec, target),
             device_id_type=MESH,
         )
@@ -130,8 +135,9 @@
             device_id_type=MESH,
         )
 
-    for side in range(2):
-        halo(0, side).start()
+    for part in range(EDGE_PARTS):
+        for side in range(2):
+            halo(0, side, part).start()
     for k in range(1, n_dom):
         code_copy(k).start()
     in_codes[dom] = code_ref[dom]
@@ -139,13 +145,20 @@
     loads[1].wait()
 
     def add_surface(block, carry):
-        start = block * 8
-        own = buf0[pl.ds(rim + start, 8)].astype(jnp.float32)[:, :field_count]
-        mixed = flux_ref[pl.ds(start, 8)].astype(jnp.float32) + own
-        flux_ref[pl.ds(start, 8)] = mixed.astype(jnp.bfloat16)
+        start = pl.multiple_of(block * 16, 16)
+        own = buf0[pl.ds(rim + start, 16)].astype(jnp.float32)[:, :field_count]
+        by_field = flux_ref[:, pl.ds(start, 16), :].reshape(field_count * 16, cells)
+        by_tile = lax.dot_general(
+            perm_ref[...],
+            by_field,
+            (((0,), (0,)), ((), ())),
+            preferred_element_type=jnp.float32,
+        )
+        mixed = by_tile.reshape(16, field_count, cells) + own
+        field_ref[pl.ds(start, 16)] = mixed.astype(jnp.bfloat16)
         return carry
 
-    lax.fori_loop(0, tiles // 8, add_surface, 0)
+    lax.fori_loop(0, tiles // 16, add_surface, 0)
     loads[2].wait()
 
     def make_pieces(target, chunk, store):
@@ -154,7 +167,7 @@
             entry = entry_ref[target * cap + chunk * 16 + i]
             rows.append(
                 jnp.dot(
-                    flux_ref[entry // per_tile],
+                    field_ref[entry // per_tile],
                     weight_ref[entry],
                     preferred_element_type=jnp.float32,
                 )
@@ -177,7 +190,8 @@
         piece_copy(k).start()
         return carry
 
-    lax.fori_loop(1, n_dom, send_pieces, 0)
+    early = 1 + n_dom * EARLY // 8
+    lax.fori_loop(1, early, send_pieces, 0)
 
     def own_body(chunk, inner):
         def store(at, value):
@@ -186,7 +200,6 @@
         make_pieces(dom, chunk, store)
         return inner
 
-    lax.fori_loop(0, cap // 16, own_body, 0)
     loads[3].wait()
 
     def advance(step, first, count):
@@ -197,7 +210,7 @@
             for i in range(GROUP):
                 for k in range(slots_near):
                     lhs_ref[i * levels : (i + 1) * levels, k * cells : (k + 1) * cells] = source[
-                        near_ref[(start + i) * slots_near + k]
+                        near_ref[k * tiles + start + i]
                     ]
             summed = jnp.dot(lhs_ref[...], stencil_ref[...], preferred_element_type=jnp.float32)
             summed = summed.reshape(GROUP, levels, cells)
@@ -256,17 +269,22 @@
                 part_copy(target, 0, target).start()
 
     for step in range(STEPS):
-        for side in range(2):
-            halo(step, side).wait()
+        for part in range(EDGE_PARTS):
+            for side in range(2):
+                halo(step, side, part).wait()
         if step < STEPS - 1:
-            advance(step, 0, rim)
-            halo(step + 1, 0).start()
-            advance(step, tiles - rim, rim)
-            halo(step + 1, 1).start()
+            size = rim // EDGE_PARTS
+            for part in range(EDGE_PARTS):
+                for side in range(2):
+                    advance(step, side * (tiles - rim) + part * size, size)
+                    halo(step + 1, side, part).start()
             advance(step, rim, tiles - 2 * rim)
         else:
             advance(step, 0, tiles)
         if step == 0:
+            lax.fori_loop(early, n_dom, send_pieces, 0)
+            lax.fori_loop(0, cap // 16, own_body, 0)
+        if step == 1:
             exchange_sections()
 
     @pl.when(sec != last)
@@ -305,7 +323,8 @@
     placed = column * cap + jnp.sum(earlier.astype(jnp.int32), axis=1)
     slot_count = n_dom * cap
     hit = jnp.arange(slot_count, dtype=jnp.int32)[:, None] == placed[None, :]
-    packed = order * (2 * n_sec * tiles) + local_code + 1
+    origin = order % tiles * (total // tiles) + order // tiles
+    packed = origin * (2 * n_sec * tiles) + local_code + 1
     found = jnp.sum(jnp.where(hit, packed[None, :], 0), axis=1)
     entry = found // (2 * n_sec * tiles)
     code = found % (2 * n_sec * tiles) - 1
@@ -334,7 +353,7 @@
     total = tiles * per_tile
     cap = max(16, -(-total // n_dom))
     rim = tiles // 4
-    entry, codes = slot_tables(remap_pairs[0], tiles, n_dom, n_sec, cap)
+    entry, codes = slot_tables(remap_pairs[0].T, tiles, n_dom, n_sec, cap)
     rows = field_count * 16
     at = np.arange(rows)
     perm = np.zeros((rows, rows), np.float32)
@@ -355,6 +374,7 @@
         scratch_shapes=[extended] * STEPS
         + [
             pltpu.VMEM((tiles, levels, cells), jnp.bfloat16),
+            pltpu.VMEM((field_count, tiles, cells), jnp.bfloat16),
             pltpu.VMEM((tiles, field_count, cells), jnp.bfloat16),
             pltpu.VMEM((total, cells, cells), jnp.bfloat16),
             pltpu.VMEM((GROUP * levels, near * cells), jnp.bfloat16),
@@ -365,8 +385,8 @@
             pltpu.VMEM((n_sec - 1, field_count, tiles, cells), jnp.bfloat16),
             pltpu.VMEM((n_sec - 1, field_count, tiles, cells), jnp.bfloat16),
             dma((4,)),
-            dma((STEPS, 2)),
-            dma((STEPS, 2)),
+            dma((STEPS, 2 * EDGE_PARTS)),
+            dma((STEPS, 2 * EDGE_PARTS)),
             dma((n_dom,)),
             dma((n_dom,)),
             dma((n_dom,)),
@@ -378,11 +398,11 @@
             collective_id=0, has_side_effects=True, vmem_limit_bytes=56 * 2**20
         ),
     )(
-        neighbours.reshape(tiles * near),
+        neighbours[0].T.reshape(near * tiles),
         entry,
         model_state[0],
         coefficient[0],
-        surface_flux[0],
+        surface_flux[0].transpose(1, 0, 2),
         remap_weights.reshape(total, cells, cells),
         stencil_blocks.reshape(near * cells, cells),
         land_mask,

time: 110 us -> 105 us (0.955)
  local copies, waits for them, and re-layouts: 9.43 us -> 5.79 us
  Pallas kernels: 98 us -> 96.2 us
    unnamed x7 -> x5, local copies, waits for them, and re-layouts: 7.54 us -> 4.84 us
    pallas_call x1, Pallas kernels: 98 us -> 96.2 us  [local(): pl.pallas_call(functools.partial(coupled_kernel, n_dom, n_sec, cap), out_...]
where the time goes in v1:
time: 105 us; the launch traced here: 104 us
  Pallas kernels  96.2 us (92%)
  local copies, waits for them, and re-layouts  5.79 us (6%)
  other arithmetic  1.64 us (2%)
    pallas_call x1, Pallas kernels, local(): pl.pallas_call(functools.partial(coupled_kernel, n_dom, n_sec, cap), out_...  96.2 us
    unnamed x5, local copies, waits for them, and re-layouts  4.84 us

profile of v1, /device:TPU:15, one launch (start us, length us, event | category | flops | bytes accessed | tf_op | source)
XLA Modules:
  0.0 104.3 jit_solution(16660157823828570260)
XLA Ops:
  0.6 0.1 broadcast_in_dim.63
  0.7 0.1 broadcast_in_dim.64
  0.8 0.7 and_select_fusion.5
  1.5 0.2 convert_reduce_fusion
  1.7 0.1 select_reduce_fusion
  1.8 0.6 and_select_fusion.entry_ref
  2.4 0.1 reduce_sum.22
  2.5 1.3 %copy.13 = s32[1,128,7]{1,2,0:T(8,128)} copy(s32[1,128,7]{1,0,2:T(1,128)} %param.12) | data formatting | bytes 7168
  3.8 0.1 broadcast_in_dim.68
  3.9 0.6 broadcast_in_dim.70.code_ref
  4.5 96.2 %shard_map.104 = (bf16[128,48,128]{2,1,0:T(8,128)(2,1)}, bf16[20,128,128]{2,1,0:T(8,128)(2,1)}) custom-call(s32[896]{0:T(1024)} %bitcast.47, s32[256]{0:T(256)} %and_select_fusion.entry_ref, bf16[128,48,128]{2,1,0:T(8,128)(2,1)} %bitcast.41, bf16[128,48,128]{2,1,0:T(8,128)(2,1)} %bitcast.42, bf16[20,128,128]{2,1,0:T(8,128)(2,1)} %bitcast.44, ...), custom_call_target="tpu_custom_call" | custom-call | tf_op jit(solution)/shard_map/pallas_call | solution.py:366
  100.8 0.0 copy-start
  100.8 2.7 %copy.16 = bf16[1,128,48,128]{3,2,1,0:T(8,128)(2,1)} copy(bf16[1,128,48,128]{3,2,1,0:T(8,128)(2,1)} %bitcast.43) | data formatting | bytes 3145728
  103.5 0.0 copy-done
  103.5 0.8 copy.17
  (5 shorter events, 0.0 us)
Async XLA Ops:
  100.8 2.7 %copy-start = (bf16[20,128,128]{2,1,0:T(8,128)(2,1)S(1)}, bf16[20,128,128]{2,1,0:T(8,128)(2,1)}, u32[]{:S(2)}) copy-start(bf16[20,128,128]{2,1,0:T(8,128)(2,1)} %get-tuple-element.5) | copy-start | bytes 1966084
